TPU v7x, 128 devices: a whole 4x4x4 slice. The times are simulated.
128 devices in a mesh: node: 4 (over x), surf: 32 (over z, y, core).
Axes of the slice: x: 4, y: 4, z: 4, core: 2. Of those that a mesh axis runs over, the one named last changes fastest.
Arguments:
- sens: bfloat16 [256, 3, 524288], P('node', None, 'surf'), may hold values from -6 to 6
- psi: float32 [35, 256], replicated, may hold values from -4 to 4
- quad_table: float32 [16], replicated, may hold values from 0.004 to 0.04
- quad_index: int32 [256], replicated, may hold values from 0 to 15
- counts: int32 [1024], P('surf'), may hold values from 1 to 512, 327680 in all
- cells: int32 [1024], P('surf'), may hold values from 0 to 383, as said below
- coords: float32 [3, 524288], P(None, 'surf'), may hold values from 0 to 1
Outputs:
- gradient: float32 [105, 24576], P(None, ('node', 'surf'))
Inputs may be any that keep to these rules, and one draw needn't show every extreme that they name: `counts`: some patch is full, with 512 live points, in every draw. `cells`: cell e belongs to owner e // 3. Within each aligned block of 8 patches, no two patches have the same owner.
All inputs are finite; a program needn't handle non-finite values. No bound on the sum of `counts` on one device may be relied on, other than what follows from the above.
Results may differ from a plain program's by a relative error of at most 0.003.
Values may be sent and summed in bfloat16 or wider, within the bound.
No kernel may reach another device: no remote copies, remote signals or barrier semaphores. Data moves between devices by JAX's collectives and lax.ppermute only.
A program may use at most 128 MiB of HBM per device.

v0:
```python
import jax
import jax.numpy as jnp
from jax import lax
from jax.sharding import PartitionSpec as P

K = 35
NQW = 16
CELLS = 384
PATCH_PTS = 512


def bernstein(coords, live):
    one = 1.0 - coords
    basis = jnp.stack(
        [
            one * one * one,
            3.0 * coords * one * one,
            3.0 * coords * coords * one,
            coords * coords * coords,
        ],
        axis=1,
    )
    weights = basis[0][:, None, None, :] * basis[1][None, :, None, :] * basis[2][None, None, :, :]
    return weights.reshape(64, -1) * live[None, :]


def patch_tiles(chaos, counts, coords):
    npatch = counts.shape[0]
    slots = jnp.arange(PATCH_PTS, dtype=jnp.int32)
    live = (slots[None, :] < counts[:, None]).astype(jnp.float32).reshape(-1)
    bern = bernstein(coords, live).reshape(64, npatch, PATCH_PTS)
    flat = chaos.reshape(3 * K, npatch, PATCH_PTS)
    return jnp.einsum("apn,tpn->pat", flat, bern, precision=lax.Precision.HIGHEST)


def dense_lattice(tiles, cells):
    hits = (cells[:, None] == jnp.arange(CELLS, dtype=jnp.int32)[None, :]).astype(jnp.float32)
    spread = jnp.einsum("pe,pat->aet", hits, tiles, precision=lax.Precision.HIGHEST)
    partial_lattice = spread.reshape(3 * K, CELLS * 64)
    return lax.psum_scatter(partial_lattice, ("node", "surf"), scatter_dimension=1, tiled=True)


def local(sens, psi, quad_table, quad_index, counts, cells, coords):
    groups = lax.axis_size("node")
    group_index = lax.axis_index("node")
    hits = (quad_index[:, None] == jnp.arange(NQW, dtype=jnp.int32)[None, :]).astype(jnp.float32)
    qweight = jnp.dot(hits, quad_table, precision=lax.Precision.HIGHEST)
    coef = (psi * qweight[None, :]).astype(jnp.bfloat16)
    quarter_patches = counts.shape[0] // groups
    quarter_points = quarter_patches * PATCH_PTS
    pstart = group_index * quarter_patches
    qstart = group_index * quarter_points
    own_counts = lax.dynamic_slice_in_dim(counts, pstart, quarter_patches, 0)
    own_cells = lax.dynamic_slice_in_dim(cells, pstart, quarter_patches, 0)
    own_coords = lax.dynamic_slice_in_dim(coords, qstart, quarter_points, 1)
    chaos = jnp.einsum(
        "kq,qcn->kcn",
        coef,
        lax.all_to_all(sens, "node", split_axis=2, concat_axis=0, tiled=True),
        preferred_element_type=jnp.float32,
    )
    tiles = patch_tiles(chaos, own_counts, own_coords)
    return dense_lattice(tiles, own_cells)


def solution(mesh):
    in_specs = (P("node", None, "surf"), P(), P(), P(), P("surf"), P("surf"), P(None, "surf"))
    out_specs = P(None, ("node", "surf"))
    return jax.shard_map(local, mesh=mesh, in_specs=in_specs, out_specs=out_specs, check_vma=False)
```

profile of v0, /device:TPU:0, one launch (start us, length us, event | category | flops | bytes accessed | tf_op | source)
XLA Modules:
  0.0 415.6 jit_solution(15547998422458433283)
XLA Ops:
  6.5 0.0 copy-start
  6.5 20.9 %copy.18 = bf16[64,3,16384]{0,1,2:T(4,128)(2,1)} copy(bf16[64,3,16384]{2,0,1:T(8,128)(2,1)} %param.7) | data formatting | bytes 12582912 | tf_op args[0]
  27.5 14.5 %reshape.49 = bf16[4,2,393216]{2,1,0:T(2,128)(2,1)} reshape(bf16[16384,3,64]{2,1,0:T(4,128)(2,1)} %bitcast.37) | data formatting | bytes 12582912
  42.0 0.0 copy-start.4
  42.0 0.0 copy-start.5
  42.0 0.0 copy-start.3
  42.0 5.4 %all-to-all-start = ((bf16[4,2,393216]{2,1,0:T(2,128)(2,1)}), bf16[4,2,393216]{2,1,0:T(2,128)(2,1)}, u32[]{:S(2)}, u32[]{:S(2)}) async-start(bf16[4,2,393216]{2,1,0:T(2,128)(2,1)} %reshape.49), calls=%async_computation | async-start | bytes 12582912 | tf_op jit(solution)/shard_map/all_to_all | solution.py:59
  47.4 0.0 reduce-scatter.2.cloned.1.call-start
  47.4 0.9 fusion.6
  48.3 0.2 pad_maximum_fusion.4
  48.5 0.1 copy_bitcast_fusion
  48.6 0.1 broadcast_multiply_fusion.2
  48.7 0.3 broadcast_multiply_fusion.1
  49.0 0.7 mul.114
  49.7 0.0 copy-done.4
  49.7 0.1 dynamic_slice.10
  49.8 0.0 copy-done.5
  49.8 0.1 dynamic_slice.11
  49.9 0.0 copy-done
  49.9 0.0 copy-done.3
  49.9 0.2 fusion.3
  50.1 0.1 fusion.14
  50.1 0.2 broadcast_multiply_fusion
  50.3 68.5 %all-to-all-done = bf16[4,2,393216]{2,1,0:T(2,128)(2,1)} async-done(((bf16[4,2,393216]{2,1,0:T(2,128)(2,1)}), bf16[4,2,393216]{2,1,0:T(2,128)(2,1)}, u32[]{:S(2)}, u32[]{:S(2)}) %all-to-all-start) | async-done | bytes 6291488 | tf_op jit(solution)/shard_map/all_to_all | solution.py:59
  118.8 13.5 %reshape.50 = bf16[16384,3,64]{2,1,0:T(4,128)(2,1)} reshape(bf16[4,2,393216]{2,1,0:T(2,128)(2,1)} %all-to-all-done) | data formatting | bytes 12582912
  132.3 0.0 copy-start.2
  132.3 21.7 %copy.19 = bf16[64,3,4,4096]{3,0,2,1:T(8,128)(2,1)} copy(bf16[64,3,4,4096]{0,1,3,2:T(4,128)(2,1)} %bitcast.36) | data formatting | bytes 12582912 | tf_op jit(solution)/shard_map/all_to_all | solution.py:59
  154.0 0.0 copy-done.2
  154.0 4.0 fusion.11
  158.0 1.2 copy.20
  159.2 2.5 reshape.43
  161.7 5.1 %fusion = f32[8,105,64]{1,2,0:T(8,128)S(1)} fusion(f32[105,8,512]{2,1,0:T(8,128)} %reshape.43, f32[64,8,512]{2,1,0:T(8,128)S(1)} %broadcast_multiply_fusion), kind=kOutput, calls=%fused_computation.1 | convolution fusion | flops 330301440 | bytes 2983936 | tf_op jit(solution)/shard_map/apn,tpn->pat/dot_general | solution.py:33
  166.8 0.2 copy.23
  167.0 6.9 %convolution_bitcast_fusion = f32[105,384,64]{1,2,0:T(8,128)} fusion(f32[8,105,64]{2,0,1:T(8,128)S(1)} %copy.23, s32[8]{0:T(128)S(1)} %dynamic_slice.11), kind=kOutput, calls=%fused_computation | convolution fusion | flops 247729152 | bytes 10536992 | tf_op jit(solution)/shard_map/pe,pat->aet/dot_general | solution.py:38
  173.9 12.1 %copy.24 = f32[105,384,64]{0,2,1:T(8,128)} copy(f32[105,384,64]{1,2,0:T(8,128)} %convolution_bitcast_fusion) | data formatting | bytes 20643840 | tf_op jit(solution)/shard_map/pe,pat->aet/transpose | solution.py:38
  186.0 0.0 copy-start.1
  186.0 0.0 reduce-scatter.2.cloned.1.call-update
  186.0 222.7 %reduce-scatter.2.cloned.1.call-done = f32[105,192]{0,1:T(8,128)} async-done(((f32[105,24576]{0,1:T(8,128)}), f32[105,192]{0,1:T(8,128)}) %reduce-scatter.2.cloned.1.call-update) | async-done | bytes 80656 | tf_op jit(solution)/shard_map/reduce_scatter | solution.py:40
  408.8 0.0 copy-done.1
  (1 shorter events, 0.0 us)
Async XLA Ops:
  6.5 43.3 %copy-start = (f32[16]{0:T(128)S(1)}, f32[16]{0:T(128)}, u32[]{:S(2)}) copy-start(f32[16]{0:T(128)} %param.9) | copy-start | bytes 196
  42.0 7.7 %copy-start.4 = (s32[32]{0:T(128)S(1)}, s32[32]{0:T(128)}, u32[]{:S(2)}) copy-start(s32[32]{0:T(128)} %param.11) | copy-start | bytes 388
  42.0 7.8 %copy-start.5 = (s32[32]{0:T(128)S(1)}, s32[32]{0:T(128)}, u32[]{:S(2)}) copy-start(s32[32]{0:T(128)} %param.12) | copy-start | bytes 388
  42.0 7.9 %copy-start.3 = (s32[256]{0:T(256)S(1)}, s32[256]{0:T(256)}, u32[]{:S(2)}) copy-start(s32[256]{0:T(256)} %param.10) | copy-start | bytes 3076
  42.0 76.9 %all-to-all-start = ((bf16[4,2,393216]{2,1,0:T(2,128)(2,1)}), bf16[4,2,393216]{2,1,0:T(2,128)(2,1)}, u32[]{:S(2)}, u32[]{:S(2)}) async-start(bf16[4,2,393216]{2,1,0:T(2,128)(2,1)} %reshape.49), calls=%async_computation | async-start | bytes 12582912 | tf_op jit(solution)/shard_map/all_to_all | solution.py:59
  47.4 361.4 %reduce-scatter.2.cloned.1.call-start = ((), (), s32[]{:S(2)}) async-start(), calls=%async_computation.2 | async-start | bytes 12681216 | tf_op jit(solution)/shard_map/reduce_scatter | solution.py:40
  132.3 21.7 %copy-start.2 = (f32[35,256]{1,0:T(8,128)S(1)}, f32[35,256]{1,0:T(8,128)}, u32[]{:S(2)}) copy-start(f32[35,256]{1,0:T(8,128)} %param.8) | copy-start | bytes 107524
  186.0 222.8 %copy-start.1 = (f32[16]{0:T(128)S(1)}, f32[16]{0:T(128)}, u32[]{:S(2)}) copy-start(f32[16]{0:T(128)} %param.9) | copy-start | bytes 196
Sparse Core Ops, SparseCore 0:
  186.1 222.5 reduce-scatter.1
where the time goes:
time: 417 us; the launch traced here: 416 us
  waiting for transfers between devices  291 us (70%)
  local copies, waits for them, and re-layouts  87.6 us (21%)
  matrix products  16.2 us (4%)
  between operations  13.5 us (3%)
  starting transfers between devices  5.43 us (1%)
    reduce_scatter x1, waiting for transfers between devices, dense_lattice(): lax.psum_scatter(partial_lattice, ('node', 'surf'), scatter_dimension=1,...  223 us
    all_to_all x1, waiting for transfers between devices, local(): lax.all_to_all(sens, 'node', split_axis=2, concat_axis=0, tiled=True)  68.5 us
    unnamed x17, local copies, waits for them, and re-layouts  49.1 us
    all_to_all x1, local copies, waits for them, and re-layouts, local(): lax.all_to_all(sens, 'node', split_axis=2, concat_axis=0, tiled=True)  21.7 us
    transpose x1, local copies, waits for them, and re-layouts, dense_lattice(): jnp.einsum('pe,pat->aet', hits, tiles, precision=lax.Precision.HIGHEST)  12.1 us
  transfers between devices with their start and end apart: 2, of which 2 were waited for; matrix products, arithmetic and copies ran while one was open for 1% of the time, Pallas kernels for 0%

commit v1 on v0

--- a/solution.py
+++ b/solution.py
@@ -7,6 +7,15 @@
 NQW = 16
 CELLS = 384
 PATCH_PTS = 512
+
+
+def _search_streams(obj, ndim_at, along_dim):
+    return jnp.concatenate(
+        lax.all_to_all(
+            jnp.stack(jnp.split(obj, lax.axis_size("node"), axis=ndim_at)), "node", 0, 0
+        ),
+        axis=along_dim,
+    )
 
 
 def bernstein(coords, live):
@@ -54,10 +63,7 @@
     own_cells = lax.dynamic_slice_in_dim(cells, pstart, quarter_patches, 0)
     own_coords = lax.dynamic_slice_in_dim(coords, qstart, quarter_points, 1)
     chaos = jnp.einsum(
-        "kq,qcn->kcn",
-        coef,
-        lax.all_to_all(sens, "node", split_axis=2, concat_axis=0, tiled=True),
-        preferred_element_type=jnp.float32,
+        "kq,qcn->kcn", coef, _search_streams(sens, 2, 0), preferred_element_type=jnp.float32
     )
     tiles = patch_tiles(chaos, own_counts, own_coords)
     return dense_lattice(tiles, own_cells)

time: 417 us -> 352 us (0.84)
  local copies, waits for them, and re-layouts: 87.6 us -> 23.5 us
    unnamed x17 -> x12, local copies, waits for them, and re-layouts: 49.1 us -> 0.16 us
    all_to_all x1, local copies, waits for them, and re-layouts: 21.7 us -> 3.21 us  [_search_streams(): lax.all_to_all(jnp.stack(jnp.split(obj, lax.axis_size('node'), axis=ndim_...]
where the time goes in v1:
time: 352 us
  waiting for transfers between devices  291 us (83%)
  local copies, waits for them, and re-layouts  23.5 us (7%)
  between operations  13.5 us (4%)
  matrix products  13.4 us (4%)
  starting transfers between devices  5.41 us (2%)
  other arithmetic  4.82 us (1%)
    reduce_scatter x1, waiting for transfers between devices, dense_lattice(): lax.psum_scatter(partial_lattice, ('node', 'surf'), scatter_dimension=1,...  223 us
    all_to_all x1, waiting for transfers between devices, _search_streams(): lax.all_to_all(jnp.stack(jnp.split(obj, lax.axis_size('node'), axis=ndim_...  68.5 us
    transpose x1, local copies, waits for them, and re-layouts, dense_lattice(): jnp.einsum('pe,pat->aet', hits, tiles, precision=lax.Precision.HIGHEST)  12.1 us
  transfers between devices with their start and end apart: 2, of which 2 were waited for; matrix products, arithmetic and copies ran while one was open for 1% of the time, Pallas kernels for 0%

profile of v1, /device:TPU:0, one launch (start us, length us, event | category | flops | bytes accessed | tf_op | source)
XLA Modules:
  0.0 351.9 jit_solution(1548785659387947361)
XLA Ops:
  6.5 0.0 copy-start
  6.5 3.3 slice_bitcast_fusion.3
  9.8 3.2 pad_maximum_fusion
  13.0 0.0 copy-start.3
  13.0 0.0 copy-start.4
  13.0 5.4 %all-to-all-start = ((bf16[4,64,3,4096]{3,1,2,0:T(8,128)(2,1)}), bf16[4,64,3,4096]{3,1,2,0:T(8,128)(2,1)}, u32[]{:S(2)}, u32[]{:S(2)}) async-start(bf16[4,64,3,4096]{3,1,2,0:T(8,128)(2,1)} %pad_maximum_fusion), calls=%async_computation | async-start | bytes 12582912 | tf_op jit(solution)/shard_map/all_to_all | solution.py:14
  18.4 0.0 reduce-scatter.2.cloned.1.call-start
  18.5 0.0 copy-done.3
  18.5 0.1 dynamic_slice.10
  18.6 0.0 copy-done.4
  18.6 0.1 dynamic_slice.11
  18.6 0.9 fusion.6
  19.5 0.0 copy-start.2
  19.5 0.2 pad_maximum_fusion.5
  19.8 0.1 copy_bitcast_fusion
  19.9 0.1 broadcast_multiply_fusion.2
  19.9 0.3 broadcast_multiply_fusion.1
  20.2 0.7 mul.114
  20.9 0.0 copy-done
  20.9 0.0 copy-done.2
  20.9 0.2 fusion.3
  21.1 0.1 fusion.14
  21.2 0.2 broadcast_multiply_fusion
  21.4 0.0 copy-start.1
  21.4 68.5 %all-to-all-done = bf16[4,64,3,4096]{3,1,2,0:T(8,128)(2,1)} async-done(((bf16[4,64,3,4096]{3,1,2,0:T(8,128)(2,1)}), bf16[4,64,3,4096]{3,1,2,0:T(8,128)(2,1)}, u32[]{:S(2)}, u32[]{:S(2)}) %all-to-all-start) | async-done | bytes 6291488 | tf_op jit(solution)/shard_map/all_to_all | solution.py:14
  89.9 3.2 copy.9
  93.1 0.0 copy-done.1
  93.1 1.2 fusion.11
  94.3 1.2 copy.10
  95.5 2.5 reshape.47
  98.0 5.1 %fusion = f32[8,105,64]{1,2,0:T(8,128)S(1)} fusion(f32[105,8,512]{2,1,0:T(8,128)} %reshape.47, f32[64,8,512]{2,1,0:T(8,128)S(1)} %broadcast_multiply_fusion), kind=kOutput, calls=%fused_computation.2 | convolution fusion | flops 330301440 | bytes 2983936 | tf_op jit(solution)/shard_map/apn,tpn->pat/dot_general | solution.py:42
  103.1 0.2 copy.14
  103.3 6.9 %convolution_bitcast_fusion = f32[105,384,64]{1,2,0:T(8,128)} fusion(f32[8,105,64]{2,0,1:T(8,128)S(1)} %copy.14, s32[8]{0:T(128)S(1)} %dynamic_slice.11), kind=kOutput, calls=%fused_computation.1 | convolution fusion | flops 247729152 | bytes 10536992 | tf_op jit(solution)/shard_map/pe,pat->aet/dot_general | solution.py:47
  110.2 12.1 %copy.11 = f32[105,384,64]{0,2,1:T(8,128)} copy(f32[105,384,64]{1,2,0:T(8,128)} %convolution_bitcast_fusion) | data formatting | bytes 20643840 | tf_op jit(solution)/shard_map/pe,pat->aet/transpose | solution.py:47
  122.3 0.0 reduce-scatter.2.cloned.1.call-update
  122.3 222.8 %reduce-scatter.2.cloned.1.call-done = f32[105,192]{0,1:T(8,128)} async-done(((f32[105,24576]{0,1:T(8,128)}), f32[105,192]{0,1:T(8,128)}) %reduce-scatter.2.cloned.1.call-update) | async-done | bytes 80656 | tf_op jit(solution)/shard_map/reduce_scatter | solution.py:49
  (1 shorter events, 0.0 us)
Async XLA Ops:
  6.5 14.4 %copy-start = (f32[16]{0:T(128)S(1)}, f32[16]{0:T(128)}, u32[]{:S(2)}) copy-start(f32[16]{0:T(128)} %param.9) | copy-start | bytes 196
  13.0 5.4 %copy-start.3 = (s32[32]{0:T(128)S(1)}, s32[32]{0:T(128)}, u32[]{:S(2)}) copy-start(s32[32]{0:T(128)} %param.11) | copy-start | bytes 388
  13.0 5.5 %copy-start.4 = (s32[32]{0:T(128)S(1)}, s32[32]{0:T(128)}, u32[]{:S(2)}) copy-start(s32[32]{0:T(128)} %param.12) | copy-start | bytes 388
  13.0 76.8 %all-to-all-start = ((bf16[4,64,3,4096]{3,1,2,0:T(8,128)(2,1)}), bf16[4,64,3,4096]{3,1,2,0:T(8,128)(2,1)}, u32[]{:S(2)}, u32[]{:S(2)}) async-start(bf16[4,64,3,4096]{3,1,2,0:T(8,128)(2,1)} %pad_maximum_fusion), calls=%async_computation | async-start | bytes 12582912 | tf_op jit(solution)/shard_map/all_to_all | solution.py:14
  18.4 326.6 %reduce-scatter.2.cloned.1.call-start = ((), (), s32[]{:S(2)}) async-start(), calls=%async_computation.2 | async-start | bytes 12681216 | tf_op jit(solution)/shard_map/reduce_scatter | solution.py:49
  19.5 1.4 copy-start.2
  21.4 71.7 %copy-start.1 = (f32[35,256]{1,0:T(8,128)S(1)}, f32[35,256]{1,0:T(8,128)}, u32[]{:S(2)}) copy-start(f32[35,256]{1,0:T(8,128)} %param.8) | copy-start | bytes 107524
Sparse Core Ops, SparseCore 0:
  122.4 222.5 reduce-scatter.1
